TPU v7x, 256 devices: a whole 4x4x8 slice. The times are simulated.
256 devices in a mesh: dp: 16 (over x_hi, y, core), tensor: 16 (over x_lo, z).
Axes of the slice: x: 4 (x_hi: 2, x_lo: 2; x = x_hi * 2 + x_lo), y: 4, z: 8, core: 2. Of those that a mesh axis runs over, the one named last changes fastest.
Arguments:
- tokens: bfloat16 [4096, 4096], P(('dp', 'tensor')), may hold values from -24 to 24
- gate_weight: bfloat16 [4096, 14336], P('dp', 'tensor'), may hold values from -0.09375 to 0.09375
- up_weight: bfloat16 [4096, 14336], P('dp', 'tensor'), may hold values from -0.09375 to 0.09375
- hidden_cotangent: bfloat16 [4096, 14336], P('dp', 'tensor'), may hold values from -1.5 to 1.5
Outputs:
- hidden: bfloat16 [4096, 14336], P('dp', 'tensor')
- grad_tokens: bfloat16 [4096, 4096], P(('dp', 'tensor'))
- grad_gate: bfloat16 [4096, 14336], P('dp', 'tensor')
- grad_up: bfloat16 [4096, 14336], P('dp', 'tensor')
All inputs are finite; a program needn't handle non-finite values.
Results may differ from a plain program's by a relative error of at most 0.023.
Values may be sent and summed in bfloat16 or wider, within the bound.
A program may use at most 64 MiB of HBM per device.

v0:
```python
import jax
import jax.numpy as jnp
from jax import lax
from jax.sharding import Mesh
from jax.sharding import PartitionSpec as P

SPLIT = ("xh", "c")
TENSOR = ("xl", "z")
DP = ("xh", "y", "c")
ROWS = P((*DP, *TENSOR), None)
BLOCK = P(DP, TENSOR)


def swiglu_parts(gate_pre, up_pre, cotangent):
    sigmoid_val = jax.nn.sigmoid(gate_pre)
    activation = gate_pre * sigmoid_val
    hidden = (activation * up_pre).astype(jnp.bfloat16)
    upstream = cotangent.astype(jnp.float32)
    slope = sigmoid_val * (1.0 + gate_pre * (1.0 - sigmoid_val))
    grad_gate_pre = (upstream * up_pre * slope).astype(jnp.bfloat16)
    grad_up_pre = (upstream * activation).astype(jnp.bfloat16)
    return (hidden, grad_gate_pre, grad_up_pre)


def body(tokens, gate_weight, up_weight, cotangent):
    rows, model = tokens.shape
    depth, width = gate_weight.shape
    nx, ny, nc = (lax.axis_size(a) for a in DP)
    nt = lax.axis_size(TENSOR)
    cut = tokens.reshape(rows, nx, ny, nc, depth).transpose(1, 3, 0, 2, 4)
    cut = cut.reshape(nx * nc, rows, ny * depth)
    cut = lax.all_to_all(cut, SPLIT, 0, 0, tiled=True)
    mine = lax.all_gather(cut, TENSOR, axis=1, tiled=True)
    mine = mine.reshape(nx * nc * nt * rows, ny * depth)
    weights = lax.all_gather(
        jnp.concatenate([gate_weight, up_weight], axis=1), "y", axis=0, tiled=True
    )
    part = jnp.dot(mine, weights, preferred_element_type=jnp.float32).astype(jnp.bfloat16)
    pre = lax.psum_scatter(part, SPLIT, scatter_dimension=0, tiled=True).astype(jnp.float32)
    hidden, grad_gate_pre, grad_up_pre = swiglu_parts(pre[:, :width], pre[:, width:], cotangent)
    grads = lax.all_gather(
        jnp.concatenate([grad_gate_pre, grad_up_pre], axis=1), SPLIT, axis=0, tiled=True
    )
    back = lax.dot_general(
        grads, weights, (((1,), (1,)), ((), ())), preferred_element_type=jnp.float32
    ).astype(jnp.bfloat16)
    nl, nz = (lax.axis_size(a) for a in TENSOR)
    back = back.reshape(nx * nc, nl, nz, rows, ny * depth).transpose(2, 1, 0, 3, 4)
    back = lax.psum_scatter(back, "z", scatter_dimension=0, tiled=True)[0]
    back = lax.psum_scatter(back, "xl", scatter_dimension=0, tiled=True)[0]
    back = lax.all_to_all(back, SPLIT, 0, 0, tiled=True)
    back = back.reshape(nx, nc, rows, ny, depth).transpose(2, 0, 3, 1, 4).reshape(rows, model)
    total = lax.dot_general(
        mine, grads, (((0,), (0,)), ((), ())), preferred_element_type=jnp.float32
    ).astype(jnp.bfloat16)
    total = lax.psum_scatter(total, "y", scatter_dimension=0, tiled=True)
    return (hidden, back, total[:, :width], total[:, width:])


def solution(mesh):
    torus = Mesh(mesh.devices.reshape(2, 4, 2, 2, 8), (*DP, *TENSOR))
    specs = (ROWS, BLOCK, BLOCK, BLOCK)
    outs = (BLOCK, ROWS, BLOCK, BLOCK)
    return jax.shard_map(body, mesh=torus, in_specs=specs, out_specs=outs, check_vma=False)
```

profile of v0, /device:TPU:1, one launch (start us, length us, event | category | flops | bytes accessed | tf_op | source)
XLA Modules:
  0.0 426.6 jit_solution(17104382645673480068)
XLA Ops:
  7.2 0.0 all-gather.6.cloned.1.call-start
  7.2 1.0 reshape.26
  8.2 0.1 copy.30
  8.3 0.1 reshape.27
  8.3 11.4 %all_to_all.10 = bf16[4,16,1024]{2,1,0:T(8,128)(2,1)} all-to-all(bf16[4,16,1024]{2,1,0:T(8,128)(2,1)S(1)} %reshape.27), channel_id=1, replica_groups=mesh['xh'=2,'y'=4,'c'=2,'xl'=2,'z'=8] {'xh','c'}, dimensions={0} | all-to-all | bytes 262144 | tf_op jit(solution)/shard_map/all_to_all | solution.py:32
  19.7 0.0 all-gather.6.cloned.1.call-update
  19.7 0.0 all-gather.4.cloned.1.call-start
  19.8 2.2 pad_maximum_fusion
  22.0 0.0 all-gather.4.cloned.1.call-update
  22.0 0.0 reduce-scatter.9.cloned.1.call-start
  22.0 60.2 %all-gather.6.cloned.1.call-done = bf16[4,256,1024]{2,1,0:T(8,128)(2,1)} async-done(((bf16[4,16,1024]{2,1,0:T(8,128)(2,1)}), bf16[4,256,1024]{2,1,0:T(8,128)(2,1)}) %all-gather.6.cloned.1.call-update) | async-done | bytes 2097168 | tf_op jit(solution)/shard_map/all_gather | solution.py:33
  82.2 55.2 %all-gather.4.cloned.1.call-done = bf16[1024,1792]{1,0:T(8,128)(2,1)} async-done(((bf16[256,1792]{1,0:T(8,128)(2,1)}), bf16[1024,1792]{1,0:T(8,128)(2,1)}) %all-gather.4.cloned.1.call-update) | async-done | bytes 3670032 | tf_op jit(solution)/shard_map/all_gather | solution.py:35
  137.4 8.6 %fusion = bf16[1024,1792]{0,1:T(8,128)(2,1)} fusion(bf16[1024,1792]{1,0:T(8,128)(2,1)} %all-gather.4.cloned.1.call-done, bf16[1024,1024]{1,0:T(8,128)(2,1)} %bitcast.41), kind=kOutput, calls=%fused_computation.2 | convolution fusion | flops 3759931392 | bytes 9437184 | tf_op jit(solution)/shard_map/dot_general | solution.py:38
  146.0 0.0 copy-start
  146.0 0.0 reduce-scatter.9.cloned.1.call-update
  146.0 0.0 all-gather.8.cloned.1.call-start
  146.0 0.9 copy-done
  147.0 0.2 copy.20
  147.2 52.5 %reduce-scatter.9.cloned.1.call-done = bf16[256,1792]{0,1:T(8,128)(2,1)} async-done(((bf16[1024,1792]{0,1:T(8,128)(2,1)}), bf16[256,1792]{0,1:T(8,128)(2,1)}) %reduce-scatter.9.cloned.1.call-update) | async-done | bytes 917520 | tf_op jit(solution)/shard_map/reduce_scatter | solution.py:39
  199.7 1.3 convert_element_type.32
  201.0 0.7 fusion.3
  201.7 1.0 pad_maximum_fusion.1
  202.6 0.0 all-gather.8.cloned.1.call-update
  202.7 0.0 copy-start.3
  202.7 0.0 copy-start.1
  202.7 0.0 all-reduce.5.cloned.1.call-start
  202.7 38.6 %all-gather.8.cloned.1.call-done = bf16[1024,1792]{0,1:T(8,128)(2,1)} async-done(((bf16[256,1792]{0,1:T(8,128)(2,1)}), bf16[1024,1792]{0,1:T(8,128)(2,1)}) %all-gather.8.cloned.1.call-update) | async-done | bytes 3670032 | tf_op jit(solution)/shard_map/all_gather | solution.py:41
  241.3 8.5 %convolution_convert_fusion.2 = bf16[1024,1024]{1,0:T(8,128)(2,1)} fusion(bf16[1024,1792]{0,1:T(8,128)(2,1)} %all-gather.8.cloned.1.call-done, bf16[1024,1792]{1,0:T(8,128)(2,1)} %all-gather.4.cloned.1.call-done), kind=kOutput, calls=%fused_computation.4 | convolution fusion | flops 3759144960 | bytes 9437184 | tf_op jit(solution)/shard_map/dot_general | solution.py:44
  249.8 0.0 all-reduce.5.cloned.1.call-update
  249.8 0.0 all-reduce.7.cloned.1.call-start
  249.9 0.0 copy-done.3
  249.9 0.6 dynamic-slice
  250.5 77.4 %all-reduce.5.cloned.1.call-done = bf16[8,2,4,16,1024]{4,3,0,1,2:T(8,128)(2,1)} async-done(((bf16[8,2,4,16,1024]{4,3,0,1,2:T(8,128)(2,1)}), bf16[8,2,4,16,1024]{4,3,0,1,2:T(8,128)(2,1)}) %all-reduce.5.cloned.1.call-update) | async-done | bytes 2097168
  327.9 2.3 dynamic-slice_bitcast_fusion
  330.2 0.0 all-reduce.7.cloned.1.call-update
  330.2 0.2 reduce-scatter.11.cloned.1.call-start
  330.4 0.0 copy-done.1
  330.5 7.6 %fusion.1 = bf16[1024,1792]{0,1:T(8,128)(2,1)} fusion(bf16[1024,1792]{0,1:T(8,128)(2,1)} %all-gather.8.cloned.1.call-done, bf16[1024,1024]{1,0:T(8,128)(2,1)S(1)} %bitcast.42), kind=kOutput, calls=%fused_computation.3 | convolution fusion | flops 3759931392 | bytes 9437184 | tf_op jit(solution)/shard_map/dot_general | solution.py:53
  338.0 0.0 copy-start.2
  338.0 0.0 reduce-scatter.11.cloned.1.call-update
  338.1 0.7 copy-done.2
  338.7 0.6 dynamic-slice.2
  339.3 28.0 %all-reduce.7.cloned.1.call-done = bf16[2,4,16,1024]{3,2,0,1:T(8,128)(2,1)} async-done(((bf16[2,4,16,1024]{3,2,0,1:T(8,128)(2,1)}), bf16[2,4,16,1024]{3,2,0,1:T(8,128)(2,1)}) %all-reduce.7.cloned.1.call-update) | async-done | bytes 262160
  367.3 2.2 dynamic-slice_bitcast_fusion.1
  369.6 5.1 %all-to-all-start.1 = ((bf16[4,16,1024]{2,1,0:T(8,128)(2,1)}), bf16[4,16,1024]{2,1,0:T(8,128)(2,1)S(1)}, u32[]{:S(2)}, u32[]{:S(2)}) async-start(bf16[4,16,1024]{2,1,0:T(8,128)(2,1)} %dynamic-slice_bitcast_fusion.1), calls=%async_computation.2 | async-start | bytes 262144 | tf_op jit(solution)/shard_map/all_to_all | solution.py:51
  374.6 1.0 copy.22
  375.6 4.1 all-to-all-done.1
  379.7 0.1 reshape.30
  379.8 0.1 copy.21
  380.0 0.7 reshape.31
  380.7 35.8 %reduce-scatter.11.cloned.1.call-done = bf16[256,1792]{0,1:T(8,128)(2,1)} async-done(((bf16[1024,1792]{0,1:T(8,128)(2,1)}), bf16[256,1792]{0,1:T(8,128)(2,1)}) %reduce-scatter.11.cloned.1.call-update) | async-done | bytes 917520 | tf_op jit(solution)/shard_map/reduce_scatter | solution.py:56
  416.5 1.2 fusion.6
  417.8 1.0 copy.23
  418.7 1.0 copy.24
Async XLA Ops:
  7.2 75.0 %all-gather.6.cloned.1.call-start = ((), (), s32[]{:S(2)}) async-start(), calls=%async_computation.5 | async-start | bytes 2228224 | tf_op jit(solution)/shard_map/all_gather | solution.py:33
  19.7 117.6 %all-gather.4.cloned.1.call-start = ((), (), s32[]{:S(2)}) async-start(), calls=%async_computation.4 | async-start | bytes 4587520 | tf_op jit(solution)/shard_map/all_gather | solution.py:35
  22.0 177.7 %reduce-scatter.9.cloned.1.call-start = ((), (), s32[]{:S(2)}) async-start(), calls=%async_computation.6 | async-start | bytes 4587520 | tf_op jit(solution)/shard_map/reduce_scatter | solution.py:39
  146.0 1.0 copy-start
  146.0 95.3 %all-gather.8.cloned.1.call-start = ((), (), s32[]{:S(2)}) async-start(), calls=%async_computation.7 | async-start | bytes 4587520 | tf_op jit(solution)/shard_map/all_gather | solution.py:41
  202.7 47.2 %copy-start.3 = (u32[256]{0:T(256)S(1)}, u32[256]{0:T(256)}, u32[]{:S(2)}) copy-start(u32[256]{0:T(256)} %constant.5) | copy-start | bytes 3076
  202.7 127.8 %copy-start.1 = (bf16[4,256,1024]{2,1,0:T(8,128)(2,1)S(1)}, bf16[4,256,1024]{2,1,0:T(8,128)(2,1)}, u32[]{:S(2)}) copy-start(bf16[4,256,1024]{2,1,0:T(8,128)(2,1)} %all-gather.6.cloned.1.call-done) | copy-start | bytes 6291460
  202.7 125.2 %all-reduce.5.cloned.1.call-start = ((), (), s32[]{:S(2)}) async-start(), calls=%async_computation.9 | async-start | bytes 4194304
  249.8 117.5 %all-reduce.7.cloned.1.call-start = ((), (), s32[]{:S(2)}) async-start(), calls=%async_computation.10 | async-start | bytes 524288
  330.2 86.3 %reduce-scatter.11.cloned.1.call-start = ((), (), s32[]{:S(2)}) async-start(), calls=%async_computation.8 | async-start | bytes 4587520 | tf_op jit(solution)/shard_map/reduce_scatter | solution.py:56
  338.0 0.7 copy-start.2
  369.6 10.2 %all-to-all-start.1 = ((bf16[4,16,1024]{2,1,0:T(8,128)(2,1)}), bf16[4,16,1024]{2,1,0:T(8,128)(2,1)S(1)}, u32[]{:S(2)}, u32[]{:S(2)}) async-start(bf16[4,16,1024]{2,1,0:T(8,128)(2,1)} %dynamic-slice_bitcast_fusion.1), calls=%async_computation.2 | async-start | bytes 262144 | tf_op jit(solution)/shard_map/all_to_all | solution.py:51
Sparse Core Ops, SparseCore 0:
  19.9 62.2 all-gather.5
  84.0 53.2 all-gather.3
  146.1 53.5 reduce-scatter.8
  202.8 38.4 all-gather.7
  249.9 77.8 all-reduce.4
  331.0 36.2 all-reduce.6
  369.9 46.6 reduce-scatter.10
where the time goes:
time: 427 us
  waiting for transfers between devices  352 us (82%)
  matrix products  24.7 us (6%)
  between operations  14.2 us (3%)
  local copies, waits for them, and re-layouts  13.7 us (3%)
  blocking collectives  11.4 us (3%)
  starting transfers between devices  5.55 us (1%)
  other arithmetic  5.14 us (1%)
    unnamed x9, waiting for transfers between devices  106 us
    all_gather x1, waiting for transfers between devices, body(): mine = lax.all_gather(cut, TENSOR, axis=1, tiled=True)  60.2 us
    all_gather x1, waiting for transfers between devices, body(): lax.all_gather(jnp.concatenate([gate_weight, up_weight], axis=1), 'y', ax...  55.2 us
    reduce_scatter x1, waiting for transfers between devices, body(): lax.psum_scatter(part, SPLIT, scatter_dimension=0, tiled=True)  52.5 us
    all_gather x1, waiting for transfers between devices, body(): lax.all_gather(jnp.concatenate([grad_gate_pre, grad_up_pre], axis=1), SPL...  38.6 us
    reduce_scatter x1, waiting for transfers between devices, body(): total = lax.psum_scatter(total, 'y', scatter_dimension=0, tiled=True)  35.8 us
    all_to_all x1, blocking collectives, body(): cut = lax.all_to_all(cut, SPLIT, 0, 0, tiled=True)  11.4 us
    dot_general x1, matrix products, body(): jnp.dot(mine, weights, preferred_element_type=jnp.float32)  8.59 us
  transfers between devices with their start and end apart: 8, of which 8 were waited for; matrix products, arithmetic and copies ran while one was open for 4% of the time, Pallas kernels for 0%

commit v1 on v0

--- a/solution.py
+++ b/solution.py
@@ -9,6 +9,13 @@
 DP = ("xh", "y", "c")
 ROWS = P((*DP, *TENSOR), None)
 BLOCK = P(DP, TENSOR)
+
+
+def exchange_gather(x, name, dim):
+    devices = lax.axis_size(name)
+    blocks = jnp.stack([x for _ in range(devices)])
+    blocks = lax.all_to_all(blocks, name, split_axis=0, concat_axis=0)
+    return jnp.concatenate(blocks, axis=dim)
 
 
 def swiglu_parts(gate_pre, up_pre, cotangent):
@@ -30,7 +37,7 @@
     cut = tokens.reshape(rows, nx, ny, nc, depth).transpose(1, 3, 0, 2, 4)
     cut = cut.reshape(nx * nc, rows, ny * depth)
     cut = lax.all_to_all(cut, SPLIT, 0, 0, tiled=True)
-    mine = lax.all_gather(cut, TENSOR, axis=1, tiled=True)
+    mine = exchange_gather(cut, TENSOR, 1)
     mine = mine.reshape(nx * nc * nt * rows, ny * depth)
     weights = lax.all_gather(
         jnp.concatenate([gate_weight, up_weight], axis=1), "y", axis=0, tiled=True

time: 427 us -> 365 us (0.85)
  waiting for transfers between devices: 352 us -> 236 us
  blocking collectives: 11.4 us -> 65.5 us
    all_gather x1 -> x0, waiting for transfers between devices: 60.2 us -> none  [body(): mine = lax.all_gather(cut, TENSOR, axis=1, tiled=True)]
    all_gather x1, waiting for transfers between devices: 55.2 us -> 0.02 us  [body(): lax.all_gather(jnp.concatenate([gate_weight, up_weight], axis=1), 'y', ax...]
    all_to_all x0 -> x1, blocking collectives: none -> 54.8 us  [exchange_gather(): blocks = lax.all_to_all(blocks, name, split_axis=0, concat_axis=0)]
    unnamed x9 -> x8, waiting for transfers between devices: 106 us -> 106 us
  transfers between devices with their start and end apart: 8 -> 7, of which waited for: 8 -> 6; matrix products, arithmetic and copies ran while one was open for 4% -> 4% of each run, Pallas kernels for 0% -> 0%
where the time goes in v1:
time: 365 us
  waiting for transfers between devices  236 us (65%)
  blocking collectives  65.5 us (18%)
  matrix products  23.8 us (7%)
  between operations  14.2 us (4%)
  local copies, waits for them, and re-layouts  14.1 us (4%)
  starting transfers between devices  5.33 us (1%)
  other arithmetic  5.18 us (1%)
    unnamed x8, waiting for transfers between devices  106 us
    all_to_all x1, blocking collectives, exchange_gather(): blocks = lax.all_to_all(blocks, name, split_axis=0, concat_axis=0)  54.8 us
    reduce_scatter x1, waiting for transfers between devices, body(): lax.psum_scatter(part, SPLIT, scatter_dimension=0, tiled=True)  52.2 us
    all_gather x1, waiting for transfers between devices, body(): lax.all_gather(jnp.concatenate([grad_gate_pre, grad_up_pre], axis=1), SPL...  38.6 us
    reduce_scatter x1, waiting for transfers between devices, body(): total = lax.psum_scatter(total, 'y', scatter_dimension=0, tiled=True)  35.7 us
    all_to_all x1, blocking collectives, body(): cut = lax.all_to_all(cut, SPLIT, 0, 0, tiled=True)  10.7 us
    dot_general x1, matrix products, body(): lax.dot_general(grads, weights, (((1,), (1,)), ((), ())), preferred_eleme...  8.57 us
    dot_general x1, matrix products, body(): jnp.dot(mine, weights, preferred_element_type=jnp.float32)  7.71 us
  transfers between devices with their start and end apart: 7, of which 6 were waited for; matrix products, arithmetic and copies ran while one was open for 4% of the time, Pallas kernels for 0%

profile of v1, /device:TPU:1, one launch (start us, length us, event | category | flops | bytes accessed | tf_op | source)
XLA Modules:
  0.0 364.6 jit_solution(9623986976378854868)
XLA Ops:
  7.2 0.0 all-gather.3.cloned.1.call-start
  7.2 2.2 pad_maximum_fusion
  9.4 0.0 all-gather.3.cloned.1.call-update
  9.4 0.0 reduce-scatter.9.cloned.1.call-start
  9.5 1.0 reshape.28
  10.4 0.1 copy.31
  10.5 0.1 reshape.29
  10.6 10.7 %all_to_all.15 = bf16[4,16,1024]{2,1,0:T(8,128)(2,1)S(1)} all-to-all(bf16[4,16,1024]{2,1,0:T(8,128)(2,1)S(1)} %reshape.29), channel_id=1, replica_groups=mesh['xh'=2,'y'=4,'c'=2,'xl'=2,'z'=8] {'xh','c'}, dimensions={0} | all-to-all | bytes 262144 | tf_op jit(solution)/shard_map/all_to_all | solution.py:39
  21.3 0.2 stack.2
  21.6 54.8 %all_to_all.16 = bf16[16,4,16,1024]{3,2,1,0:T(8,128)(2,1)S(1)} all-to-all(bf16[16,4,16,1024]{3,2,1,0:T(8,128)(2,1)S(1)} %stack.2), channel_id=1, replica_groups=mesh['xh'=2,'y'=4,'c'=2,'xl'=2,'z'=8] {'xl','z'}, dimensions={0} | all-to-all | bytes 4194304 | tf_op jit(solution)/shard_map/all_to_all | solution.py:17
  76.3 0.2 copy.20
  76.5 0.0 all-gather.3.cloned.1.call-done
  76.5 7.7 %fusion = bf16[1024,1792]{0,1:T(8,128)(2,1)} fusion(bf16[1024,1792]{1,0:T(8,128)(2,1)} %all-gather.3.cloned.1.call-done, bf16[1024,1024]{1,0:T(8,128)(2,1)S(1)} %bitcast.40), kind=kOutput, calls=%fused_computation.2 | convolution fusion | flops 3759931392 | bytes 9437184 | tf_op jit(solution)/shard_map/dot_general | solution.py:45
  84.2 0.0 copy-start
  84.2 0.0 reduce-scatter.9.cloned.1.call-update
  84.3 0.0 all-gather.5.cloned.1.call-start
  84.3 0.9 copy-done
  85.2 0.2 copy.21
  85.5 52.2 %reduce-scatter.9.cloned.1.call-done = bf16[256,1792]{0,1:T(8,128)(2,1)} async-done(((bf16[1024,1792]{0,1:T(8,128)(2,1)}), bf16[256,1792]{0,1:T(8,128)(2,1)}) %reduce-scatter.9.cloned.1.call-update) | async-done | bytes 917520 | tf_op jit(solution)/shard_map/reduce_scatter | solution.py:46
  137.7 1.3 convert_element_type.32
  139.0 0.7 fusion.3
  139.7 1.0 pad_maximum_fusion.1
  140.7 0.0 all-gather.5.cloned.1.call-update
  140.7 0.0 copy-start.2
  140.8 0.0 all-reduce.5.cloned.1.call-start
  140.8 38.6 %all-gather.5.cloned.1.call-done = bf16[1024,1792]{0,1:T(8,128)(2,1)} async-done(((bf16[256,1792]{0,1:T(8,128)(2,1)}), bf16[1024,1792]{0,1:T(8,128)(2,1)}) %all-gather.5.cloned.1.call-update) | async-done | bytes 3670032 | tf_op jit(solution)/shard_map/all_gather | solution.py:48
  179.4 8.6 %convolution_convert_fusion.2 = bf16[1024,1024]{1,0:T(8,128)(2,1)} fusion(bf16[1024,1792]{0,1:T(8,128)(2,1)} %all-gather.5.cloned.1.call-done, bf16[1024,1792]{1,0:T(8,128)(2,1)} %all-gather.3.cloned.1.call-done), kind=kOutput, calls=%fused_computation.4 | convolution fusion | flops 3759144960 | bytes 9437184 | tf_op jit(solution)/shard_map/dot_general | solution.py:51
  187.9 0.0 all-reduce.5.cloned.1.call-update
  187.9 0.0 all-reduce.7.cloned.1.call-start
  188.0 0.0 copy-done.2
  188.0 0.6 dynamic-slice
  188.6 77.5 %all-reduce.5.cloned.1.call-done = bf16[8,2,4,16,1024]{4,3,0,1,2:T(8,128)(2,1)} async-done(((bf16[8,2,4,16,1024]{4,3,0,1,2:T(8,128)(2,1)}), bf16[8,2,4,16,1024]{4,3,0,1,2:T(8,128)(2,1)}) %all-reduce.5.cloned.1.call-update) | async-done | bytes 2097168
  266.1 2.3 dynamic-slice_bitcast_fusion
  268.4 0.0 all-reduce.7.cloned.1.call-update
  268.4 0.0 reduce-scatter.11.cloned.1.call-start
  268.5 7.6 %fusion.1 = bf16[1024,1792]{0,1:T(8,128)(2,1)} fusion(bf16[1024,1792]{0,1:T(8,128)(2,1)} %all-gather.5.cloned.1.call-done, bf16[1024,1024]{1,0:T(8,128)(2,1)S(1)} %bitcast.41), kind=kOutput, calls=%fused_computation.3 | convolution fusion | flops 3759931392 | bytes 9437184 | tf_op jit(solution)/shard_map/dot_general | solution.py:60
  276.0 0.0 copy-start.1
  276.0 0.0 reduce-scatter.11.cloned.1.call-update
  276.1 0.7 copy-done.1
  276.7 0.6 dynamic-slice.2
  277.3 28.2 %all-reduce.7.cloned.1.call-done = bf16[2,4,16,1024]{3,2,0,1:T(8,128)(2,1)} async-done(((bf16[2,4,16,1024]{3,2,0,1:T(8,128)(2,1)}), bf16[2,4,16,1024]{3,2,0,1:T(8,128)(2,1)}) %all-reduce.7.cloned.1.call-update) | async-done | bytes 262160
  305.5 2.2 dynamic-slice_bitcast_fusion.1
  307.8 5.1 %all-to-all-start.2 = ((bf16[4,16,1024]{2,1,0:T(8,128)(2,1)}), bf16[4,16,1024]{2,1,0:T(8,128)(2,1)S(1)}, u32[]{:S(2)}, u32[]{:S(2)}) async-start(bf16[4,16,1024]{2,1,0:T(8,128)(2,1)} %dynamic-slice_bitcast_fusion.1), calls=%async_computation.3 | async-start | bytes 262144 | tf_op jit(solution)/shard_map/all_to_all | solution.py:58
  312.8 1.0 copy.23
  313.8 4.1 %all-to-all-done.2 = bf16[4,16,1024]{2,1,0:T(8,128)(2,1)S(1)} async-done(((bf16[4,16,1024]{2,1,0:T(8,128)(2,1)}), bf16[4,16,1024]{2,1,0:T(8,128)(2,1)S(1)}, u32[]{:S(2)}, u32[]{:S(2)}) %all-to-all-start.2) | async-done | bytes 131104 | tf_op jit(solution)/shard_map/all_to_all | solution.py:58
  317.9 0.1 reshape.32
  318.0 0.1 copy.22
  318.2 0.7 reshape.33
  318.9 35.7 %reduce-scatter.11.cloned.1.call-done = bf16[256,1792]{0,1:T(8,128)(2,1)} async-done(((bf16[1024,1792]{0,1:T(8,128)(2,1)}), bf16[256,1792]{0,1:T(8,128)(2,1)}) %reduce-scatter.11.cloned.1.call-update) | async-done | bytes 917520 | tf_op jit(solution)/shard_map/reduce_scatter | solution.py:63
  354.6 1.2 fusion.6
  355.8 1.0 copy.24
  356.8 1.0 copy.25
Async XLA Ops:
  7.2 69.3 %all-gather.3.cloned.1.call-start = ((), (), s32[]{:S(2)}) async-start(), calls=%async_computation.5 | async-start | bytes 4587520 | tf_op jit(solution)/shard_map/all_gather | solution.py:42
  9.4 128.3 %reduce-scatter.9.cloned.1.call-start = ((), (), s32[]{:S(2)}) async-start(), calls=%async_computation.6 | async-start | bytes 4587520 | tf_op jit(solution)/shard_map/reduce_scatter | solution.py:46
  84.2 1.0 copy-start
  84.3 95.1 %all-gather.5.cloned.1.call-start = ((), (), s32[]{:S(2)}) async-start(), calls=%async_computation.7 | async-start | bytes 4587520 | tf_op jit(solution)/shard_map/all_gather | solution.py:48
  140.7 47.3 %copy-start.2 = (u32[256]{0:T(256)S(1)}, u32[256]{0:T(256)}, u32[]{:S(2)}) copy-start(u32[256]{0:T(256)} %constant.5) | copy-start | bytes 3076
  140.8 125.3 %all-reduce.5.cloned.1.call-start = ((), (), s32[]{:S(2)}) async-start(), calls=%async_computation.9 | async-start | bytes 4194304
  187.9 117.6 %all-reduce.7.cloned.1.call-start = ((), (), s32[]{:S(2)}) async-start(), calls=%async_computation.10 | async-start | bytes 524288
  268.4 86.2 %reduce-scatter.11.cloned.1.call-start = ((), (), s32[]{:S(2)}) async-start(), calls=%async_computation.8 | async-start | bytes 4587520 | tf_op jit(solution)/shard_map/reduce_scatter | solution.py:63
  276.0 0.7 copy-start.1
  307.8 10.2 %all-to-all-start.2 = ((bf16[4,16,1024]{2,1,0:T(8,128)(2,1)}), bf16[4,16,1024]{2,1,0:T(8,128)(2,1)S(1)}, u32[]{:S(2)}, u32[]{:S(2)}) async-start(bf16[4,16,1024]{2,1,0:T(8,128)(2,1)} %dynamic-slice_bitcast_fusion.1), calls=%async_computation.3 | async-start | bytes 262144 | tf_op jit(solution)/shard_map/all_to_all | solution.py:58
Sparse Core Ops, SparseCore 0:
  9.8 50.2 all-gather.2
  84.4 53.2 reduce-scatter.8
  140.9 38.4 all-gather.4
  188.1 77.9 all-reduce.4
  269.3 36.2 all-reduce.6
  308.0 46.6 reduce-scatter.10
